TPU v7x, 512 devices: a whole 4x8x8 slice. The times are simulated.
512 devices in a mesh: hist: 32 (over x, y), col: 16 (over z, core).
Axes of the slice: x: 4, y: 8, z: 8, core: 2. Of those that a mesh axis runs over, the one named last changes fastest.
Arguments:
- less_row: bfloat16 [2, 128, 128, 4096], P(None, None, 'col', 'hist'), may hold values from -1.796875 to 1.796875
- less_col: bfloat16 [2, 128, 128, 4096], P(None, None, 'col', 'hist'), may hold values from -1.796875 to 1.796875
- great_row: bfloat16 [2, 128, 128, 4096], P(None, None, 'col', 'hist'), may hold values from -1.796875 to 1.796875
- great_col: bfloat16 [2, 128, 128, 4096], P(None, None, 'col', 'hist'), may hold values from -1.796875 to 1.796875
- density: float32 [2, 128, 128], replicated, may hold values from -1.8 to 1.8
- hamiltonian: float32 [128, 128], replicated, may hold values from -0.5 to 0.5
Outputs:
- less_row_out: bfloat16 [2, 128, 128, 4096], P(None, None, 'col', 'hist')
- less_col_out: bfloat16 [2, 128, 128, 4096], P(None, None, 'col', 'hist')
- great_row_out: bfloat16 [2, 128, 128, 4096], P(None, None, 'col', 'hist')
- great_col_out: bfloat16 [2, 128, 128, 4096], P(None, None, 'col', 'hist')
- density_out: float32 [2, 128, 128], replicated
All inputs are finite; a program needn't handle non-finite values.
Results may differ from a plain program's by a relative error of at most 0.033.
Values may be sent and summed in bfloat16 or wider, within the bound.
A program may use at most 64 MiB of HBM per device.

v0:
```python
import jax
import jax.numpy as jnp
from jax import lax
from jax.experimental import pallas as pl
from jax.experimental.pallas import tpu as pltpu
from jax.sharding import PartitionSpec as P

STEPS = 3


step_length = 0.1
mean_field = 2.0
coupling = 1.0


def in_one_piece(arrays, axis, split_dim, concat_dim, along):
    ends, at = ([], 0)
    for a in arrays[:-1]:
        at += a.shape[along]
        ends.append(at)
    both = jnp.concatenate(arrays, axis=along)
    return tuple(
        jnp.split(
            lax.all_to_all(both, axis, split_axis=split_dim, concat_axis=concat_dim, tiled=True),
            ends,
            axis=along,
        )
    )


def split_up(array, dim, size):
    lengths = array.shape
    parts = array.reshape(*lengths[:dim], size, lengths[dim] // size, *lengths[dim + 1 :])
    return jnp.moveaxis(parts, dim, 0)


def summed_on_arrival(array, axis, dim):
    size = lax.axis_size(axis)
    parts = lax.all_to_all(split_up(array, dim, size), axis, 0, 0, tiled=True)
    return jnp.sum(parts.astype(jnp.float32), axis=0)


def from_everyone(array, axis):
    size = lax.axis_size(axis)
    return lax.all_to_all(
        jnp.broadcast_to(array[None], (size, *array.shape)), axis, 0, 0, tiled=True
    )


def over_copies(array, axis):
    return from_everyone(array, axis).sum(axis=0)


def joined_along(parts, dim):
    parts = jnp.moveaxis(parts, 0, dim)
    lengths = parts.shape
    return parts.reshape(*lengths[:dim], lengths[dim] * lengths[dim + 1], *lengths[dim + 2 :])


def gather_directly(array, axis, dim):
    return joined_along(from_everyone(array, axis), dim)


def unitary(hamiltonian, density):
    sym_ham = 0.5 * (hamiltonian + hamiltonian.T) + mean_field * jnp.diag(jnp.diagonal(density[0]))
    halved = 0.5 * step_length * sym_ham
    squared = jnp.dot(halved, halved, precision=lax.Precision.HIGHEST)
    identity = jnp.eye(sym_ham.shape[0], dtype=jnp.float32)
    factor = jnp.linalg.cholesky(identity + squared)
    unit_real = jax.scipy.linalg.cho_solve((factor, True), identity - squared)
    unit_imag = jax.scipy.linalg.cho_solve((factor, True), -2.0 * halved)
    return (unit_real, unit_imag)


def self_energy(row_hist, col_turned):
    green_real = row_hist[0].astype(jnp.float32)
    green_imag = row_hist[1].astype(jnp.float32)
    other_real = col_turned[0].astype(jnp.float32)
    other_imag = col_turned[1].astype(jnp.float32)
    square_real = green_real * green_real - green_imag * green_imag
    square_imag = 2.0 * green_real * green_imag
    out_real = coupling * coupling * (square_real * other_real - square_imag * other_imag)
    out_imag = coupling * coupling * (square_real * other_imag + square_imag * other_real)
    return jnp.stack([out_real, out_imag]).astype(jnp.bfloat16)


def contract_pair(first, second):
    return jnp.einsum("ikt,kjt->ij", first, second, preferred_element_type=jnp.float32)


def contract(sigma, rows_block):
    real_part = contract_pair(sigma[0], rows_block[0]) - contract_pair(sigma[1], rows_block[1])
    imag_part = contract_pair(sigma[0], rows_block[1]) + contract_pair(sigma[1], rows_block[0])
    return jnp.stack([real_part, imag_part])


def rotate_density(unit_real, unit_imag, rho):
    high = lax.Precision.HIGHEST
    left_real = jnp.dot(unit_real, rho[0], precision=high) - jnp.dot(
        unit_imag, rho[1], precision=high
    )
    left_imag = jnp.dot(unit_real, rho[1], precision=high) + jnp.dot(
        unit_imag, rho[0], precision=high
    )
    out_real = jnp.dot(left_real, unit_real.T, precision=high) + jnp.dot(
        left_imag, unit_imag.T, precision=high
    )
    out_imag = jnp.dot(left_imag, unit_real.T, precision=high) - jnp.dot(
        left_real, unit_imag.T, precision=high
    )
    return jnp.stack([out_real, out_imag])


def advance_rows(low_real, low_imag, history):
    count = history.shape[1]
    hist_real = history[0].reshape(count, -1)
    hist_imag = history[1].reshape(count, -1)
    out_real = jnp.dot(low_real, hist_real, preferred_element_type=jnp.float32) - jnp.dot(
        low_imag, hist_imag, preferred_element_type=jnp.float32
    )
    out_imag = jnp.dot(low_real, hist_imag, preferred_element_type=jnp.float32) + jnp.dot(
        low_imag, hist_real, preferred_element_type=jnp.float32
    )
    return jnp.stack([out_real, out_imag]).astype(jnp.bfloat16).reshape(history.shape)


def right_pair(first, matrix):
    return jnp.einsum("imt,jm->ijt", first, matrix, preferred_element_type=jnp.float32)


def advance_cols(low_real, low_imag, rows_block):
    out_real = right_pair(rows_block[0], low_real) + right_pair(rows_block[1], low_imag)
    out_imag = right_pair(rows_block[1], low_real) - right_pair(rows_block[0], low_imag)
    return jnp.stack([out_real, out_imag]).astype(jnp.bfloat16)


def direct_steps(less_row, less_col, great_row, great_col, density, hamiltonian):
    rho = density
    rows_less, rows_great = in_one_piece((less_col, great_col), "col", 1, 2, 0)
    for step_index in range(STEPS):
        unit_real, unit_imag = unitary(hamiltonian, rho)
        sigma_less = self_energy(less_row, jnp.swapaxes(rows_great, 1, 2))
        sigma_great = self_energy(great_row, jnp.swapaxes(rows_less, 1, 2))
        partial_sum = step_length * (
            contract(sigma_great, rows_less) - contract(sigma_less, rows_great)
        )
        rotated = rotate_density(unit_real, unit_imag, rho)
        column_piece = summed_on_arrival(partial_sum.astype(jnp.bfloat16), "col", 2)
        column_piece = over_copies(column_piece, "hist")
        width = column_piece.shape[2]
        start = lax.axis_index("col") * width
        own_block = lax.dynamic_slice_in_dim(rotated, start, width, 2) + column_piece
        rho = gather_directly(own_block, "col", 2)
        low_real = unit_real.astype(jnp.bfloat16)
        low_imag = unit_imag.astype(jnp.bfloat16)
        less_row = advance_rows(low_real, low_imag, less_row)
        great_row = advance_rows(low_real, low_imag, great_row)
        rows_less = advance_cols(low_real, low_imag, rows_less)
        rows_great = advance_cols(low_real, low_imag, rows_great)
    less_col, great_col = (
        lax.all_to_all(rows_less, "col", split_axis=2, concat_axis=1, tiled=True),
        lax.all_to_all(rows_great, "col", split_axis=2, concat_axis=1, tiled=True),
    )
    return (less_row, less_col, great_row, great_col, rho)


NORB = 128
BF = jnp.bfloat16
F32 = jnp.float32
MESH = pl.DeviceIdType.MESH
COL_PEERS = [(dz, dc) for dz in (4, 3, 5, 2, 6, 1, 7) for dc in (0, 1)] + [(0, 1)]
RESIDUAL_MAX = 3e-4


def split_terms(x):
    high = x.astype(BF)
    return high, (x - high.astype(F32)).astype(BF)


def fine_dot(a, b):
    ah, al = split_terms(a)
    bh, bl = split_terms(b)

    def one(p, q):
        return jnp.dot(p, q, preferred_element_type=F32)

    return one(ah, bh) + (one(ah, bl) + one(al, bh))


def parts_of(product, at):
    rr = product[at : at + NORB, :NORB]
    ri = product[at : at + NORB, NORB:]
    ir = product[at + NORB : at + 2 * NORB, :NORB]
    ii = product[at + NORB : at + 2 * NORB, NORB:]
    return rr, ri, ir, ii


def complex_dots(lefts, right):
    rows = jnp.concatenate([x for left in lefts for x in left], axis=0)
    product = fine_dot(rows, jnp.concatenate(right, axis=1))
    outs = []
    for n in range(len(lefts)):
        rr, ri, ir, ii = parts_of(product, 2 * NORB * n)
        outs.append((rr - ii, ri + ir))
    return outs


def rotate(unit, rho):
    left = complex_dots([unit], rho)[0]
    product = fine_dot(jnp.concatenate(left, axis=0), jnp.concatenate(unit, axis=1))
    rr, ri, ir, ii = parts_of(product, 0)
    return rr + ii, ir - ri


def crank_nicolson(eye, off, diag_row, diag_col):
    inv_re_col = 1.0 / (1.0 + diag_col * diag_col)
    inv_im_col = -diag_col * inv_re_col
    inv_re_row = 1.0 / (1.0 + diag_row * diag_row)
    inv_im_row = -diag_row * inv_re_row
    power = (inv_im_col * off, -inv_re_col * off)
    total = (eye + power[0], power[1])
    power = complex_dots([power], power)[0]
    for last in (False, False, True):
        if last:
            gain = complex_dots([total], power)[0]
        else:
            following, gain = complex_dots([power, total], power)
            power = following
        total = (total[0] + gain[0], total[1] + gain[1])
    inverse = (
        total[0] * inv_re_row - total[1] * inv_im_row,
        total[0] * inv_im_row + total[1] * inv_re_row,
    )
    return (2.0 * inverse[0] - eye, 2.0 * inverse[1])


def residual_of(eye, off, diag_col, unit):
    inverse = (0.5 * (unit[0] + eye), 0.5 * unit[1])
    rows = off + eye * diag_col
    product = fine_dot(rows, jnp.concatenate(inverse, axis=1))
    rest_re = inverse[0] - product[:, NORB:] - eye
    rest_im = inverse[1] + product[:, :NORB]
    sums = jnp.sum(jnp.abs(rest_re) + jnp.abs(rest_im), axis=1, keepdims=True)
    return jnp.max(sums, axis=0, keepdims=True)


def stacked_low(unit, sign):
    low_re, low_im = unit[0].astype(BF), (sign * unit[1]).astype(BF)
    top = jnp.concatenate([low_re, -low_im], axis=1)
    bottom = jnp.concatenate([low_im, low_re], axis=1)
    return jnp.concatenate([top, bottom], axis=0)


def pair_of(ref, a, k):
    sides = []
    for kk in (k, k + 1):
        planes = [ref[a, comp, kk].reshape(NORB, NORB) for comp in (0, 1)]
        sides.append(jnp.concatenate(planes, axis=0))
    return jnp.concatenate(sides, axis=1)


def advance(weights, src, dst):
    def one(a, carry):
        for k in range(0, 8, 2):
            out = jnp.dot(weights, pair_of(src, a, k), preferred_element_type=F32).astype(BF)
            for side in (0, 1):
                for comp in (0, 1):
                    block = out[NORB * comp : NORB * (comp + 1), NORB * side : NORB * (side + 1)]
                    dst[a, comp, k + side] = block.reshape(16, 8, NORB)
        return carry

    lax.fori_loop(0, 2, one, 0)


def self_energy_block(rows, cols, sigma, a, block):
    row_re, row_im = rows[a, 0, :, block].astype(F32), rows[a, 1, :, block].astype(F32)
    col_re, col_im = cols[a, 0, :, block].astype(F32), cols[a, 1, :, block].astype(F32)
    square_re = row_re * row_re - row_im * row_im
    square_im = 2.0 * row_re * row_im
    sigma[a, 0, :, block] = (square_re * col_re - square_im * col_im).astype(BF)
    sigma[a, 1, :, block] = (square_re * col_im + square_im * col_re).astype(BF)


def self_energy_all(rows, cols, sigma):
    def one(block, carry):
        for a in (0, 1):
            self_energy_block(rows, cols, sigma, a, block)
        return carry

    lax.fori_loop(0, 16, one, 0)


def collision_of(sigma, cols):
    totals = []
    for a in (0, 1):
        total = None
        for k in range(0, 8, 2):
            term = lax.dot_general(
                pair_of(sigma, a, k),
                pair_of(cols, a, k),
                (((1,), (1,)), ((), ())),
                preferred_element_type=F32,
            )
            total = term if total is None else total + term
        totals.append(total)
    rr, ri, ir, ii = parts_of(totals[0] - totals[1], 0)
    return step_length * (rr - ii), step_length * (ri + ir)


def all_copied(ref, sem):
    pltpu.make_async_copy(ref, ref, sem).wait()


def kernel(
    less_row, less_col, great_row, great_col, rho_ref, ham_ref,
    less_row_out, less_col_out, great_row_out, great_col_out, rho_out, residual_out,
    row_in, rows0, rows1, rows2, cols0, cols1, cols2, cols3, sigma, row_back,
    scat_src, scat, mid, gath, tiny_col, tiny_hist,
    in_send, in_recv, local_sem, row_sem, out_send, out_recv, back_sem,
    scat_send, scat_recv, mid_send, mid_recv, gath_send, gath_recv, tiny_send, tiny_recv,
):
    me_col, me_hist = lax.axis_index("col"), lax.axis_index("hist")
    me_z, me_core = me_col // 2, lax.rem(me_col, 2)

    def col_peer(dz, dc):
        return lax.rem(me_z + dz, 8) * 2 + lax.rem(me_core + dc, 2)

    def hist_peers(act):
        def one(offset, carry):
            act(lax.rem(me_hist + offset, 32))
            return carry

        lax.fori_loop(1, 32, one, 0)

    def push(src, dst, send, recv, axis, peer):
        pltpu.make_async_remote_copy(
            src_ref=src, dst_ref=dst, send_sem=send, recv_sem=recv,
            device_id={axis: peer}, device_id_type=MESH,
        ).start()

    barrier = pltpu.get_barrier_semaphore()
    for dz, dc in COL_PEERS:
        pl.semaphore_signal(
            barrier, inc=1, device_id={"col": col_peer(dz, dc)}, device_id_type=MESH
        )
    hist_peers(
        lambda p: pl.semaphore_signal(barrier, inc=1, device_id={"hist": p}, device_id_type=MESH)
    )
    row_refs, col_refs = (great_row, less_row), (less_col, great_col)
    for a in (0, 1):
        pltpu.make_async_copy(row_refs[a], row_in.at[a], row_sem).start()
        pltpu.make_async_copy(
            col_refs[a].at[:, pl.ds(me_col * 8, 8)], cols0.at[a, :, :, me_col], local_sem
        ).start()
    pl.semaphore_wait(barrier, 46)

    for dz, dc in COL_PEERS:
        peer = col_peer(dz, dc)
        for a in (0, 1):
            push(
                col_refs[a].at[:, pl.ds(peer * 8, 8)], cols0.at[a, :, :, me_col],
                in_send, in_recv.at[me_col], "col", peer,
            )

    eye_at = lax.broadcasted_iota(jnp.int32, (NORB, NORB), 0) == lax.broadcasted_iota(
        jnp.int32, (NORB, NORB), 1
    )
    eye = jnp.where(eye_at, 1.0, 0.0).astype(F32)
    hamiltonian = ham_ref[...]
    halved = (0.25 * step_length) * (hamiltonian + hamiltonian.T)
    off = jnp.where(eye_at, 0.0, halved)
    mean = step_length * 0.5 * mean_field

    def diagonals(matrix):
        kept = jnp.where(eye_at, matrix, 0.0)
        return jnp.sum(kept, axis=0, keepdims=True), jnp.sum(kept, axis=1, keepdims=True)

    def unitary_of(density_re):
        row, col = diagonals(halved + mean * density_re)
        return crank_nicolson(eye, off, row, col), col

    unit1, diag1 = unitary_of(rho_ref[0])
    weight_rows1, weight_cols1 = stacked_low(unit1, 1.0), stacked_low(unit1, -1.0)
    residual = residual_of(eye, off, diag1, unit1)
    rotated1 = rotate(unit1, (rho_ref[0], rho_ref[1]))

    all_copied(row_in, row_sem)

    def turn_in(block, carry):
        for a in (0, 1):
            for comp in (0, 1):
                piece = row_in[a, comp, pl.ds(block * 8, 8)].astype(F32)
                rows0[a, comp, :, block] = jnp.swapaxes(piece, 0, 1).astype(BF)
        return carry

    lax.fori_loop(0, 16, turn_in, 0)
    advance(weight_rows1, rows0, rows1)

    all_copied(cols0.at[:, :, :, 0], local_sem)
    for a in (0, 1):
        self_energy_block(rows0, cols0, sigma, a, me_col)
    for dz, dc in COL_PEERS[::-1]:
        peer = col_peer(dz, dc)
        all_copied(cols0.at[:, :, :, 0], in_recv.at[peer])
        for a in (0, 1):
            self_energy_block(rows0, cols0, sigma, a, peer)

    def scatter_sum(r, matrix):
        for comp in (0, 1):
            scat_src[r, pl.ds(16 * comp, 16)] = matrix[comp].reshape(16, 8, NORB)
        hist_peers(
            lambda p: push(
                scat_src.at[r, p], scat.at[r, me_hist],
                scat_send.at[r], scat_recv.at[r], "hist", p,
            )
        )
        scat[r, me_hist] = scat_src[r, me_hist]

    def middle_sum(r):
        all_copied(scat.at[r, pl.ds(0, 31)], scat_recv.at[r])
        mid[r, me_col] = jnp.sum(scat[r], axis=0)
        for dz, dc in COL_PEERS:
            push(
                mid.at[r, me_col], mid.at[r, me_col],
                mid_send.at[r], mid_recv.at[r], "col", col_peer(dz, dc),
            )

    def gather_sum(r):
        all_copied(mid.at[r, pl.ds(0, 15)], mid_recv.at[r])
        gath[r, me_hist] = jnp.sum(mid[r], axis=0)
        hist_peers(
            lambda p: push(
                gath.at[r, me_hist], gath.at[r, me_hist],
                gath_send.at[r], gath_recv.at[r], "hist", p,
            )
        )

    def summed(r):
        all_copied(gath.at[r, pl.ds(0, 31)], gath_recv.at[r])
        return tuple(gath[r, pl.ds(16 * comp, 16)].reshape(NORB, NORB) for comp in (0, 1))

    scatter_sum(0, collision_of(sigma, cols0))
    advance(weight_cols1, cols0, cols1)
    self_energy_all(rows1, cols1, sigma)
    second = collision_of(sigma, cols1)
    middle_sum(0)
    tiny_col[me_col] = jnp.sum(jnp.where(eye_at, second[0], 0.0), axis=0, keepdims=True)
    for dz, dc in COL_PEERS:
        push(
            tiny_col.at[me_col], tiny_col.at[me_col],
            tiny_send.at[0], tiny_recv.at[0], "col", col_peer(dz, dc),
        )
    gather_sum(0)
    all_copied(tiny_col.at[pl.ds(0, 15)], tiny_recv.at[0])
    tiny_hist[me_hist] = jnp.sum(tiny_col[...], axis=0)
    hist_peers(
        lambda p: push(
            tiny_hist.at[me_hist], tiny_hist.at[me_hist],
            tiny_send.at[1], tiny_recv.at[1], "hist", p,
        )
    )
    first = summed(0)

    density1 = (rotated1[0] + first[0], rotated1[1] + first[1])
    unit2, diag2 = unitary_of(density1[0])
    weight_rows2, weight_cols2 = stacked_low(unit2, 1.0), stacked_low(unit2, -1.0)
    rotated2 = rotate(unit2, density1)
    all_copied(tiny_hist.at[pl.ds(0, 31)], tiny_recv.at[1])
    second_diag = jnp.sum(tiny_hist[...], axis=0)
    unit3, diag3 = unitary_of(rotated2[0] + jnp.where(eye_at, second_diag, 0.0))
    weight_rows3, weight_cols3 = stacked_low(unit3, 1.0), stacked_low(unit3, -1.0)

    advance(weight_cols2, cols1, cols2)
    advance(weight_cols3, cols2, cols3)
    col_outs, row_outs = (less_col_out, great_col_out), (great_row_out, less_row_out)
    for dz, dc in COL_PEERS:
        peer = col_peer(dz, dc)
        for a in (0, 1):
            push(
                cols3.at[a, :, :, peer], col_outs[a].at[:, pl.ds(me_col * 8, 8)],
                out_send, out_recv.at[a], "col", peer,
            )
    for a in (0, 1):
        pltpu.make_async_copy(
            cols3.at[a, :, :, me_col], col_outs[a].at[:, pl.ds(me_col * 8, 8)], local_sem
        ).start()

    advance(weight_rows2, rows1, rows2)
    self_energy_all(rows2, cols2, sigma)
    third = collision_of(sigma, cols2)
    turned = rotate(unit3, second)
    scatter_sum(1, (turned[0] + third[0], turned[1] + third[1]))
    advance(weight_rows3, rows2, rows0)
    middle_sum(1)

    def turn_out(block, carry):
        for a in (0, 1):
            for comp in (0, 1):
                piece = rows0[a, comp, :, block].astype(F32)
                row_back[a, comp, pl.ds(block * 8, 8)] = jnp.swapaxes(piece, 0, 1).astype(BF)
        return carry

    lax.fori_loop(0, 16, turn_out, 0)
    for a in (0, 1):
        pltpu.make_async_copy(row_back.at[a], row_outs[a], back_sem).start()
    gather_sum(1)
    residual = jnp.maximum(residual, residual_of(eye, off, diag2, unit2))
    residual = jnp.maximum(residual, residual_of(eye, off, diag3, unit3))
    residual_out[...] = jnp.broadcast_to(residual, (8, NORB))
    rotated3 = rotate(unit3, rotated2)
    last = summed(1)
    for comp in (0, 1):
        rho_out[comp] = rotated3[comp] + last[comp]

    for r in (0, 1):
        all_copied(scat_src.at[r, pl.ds(0, 31)], scat_send.at[r])
        all_copied(mid.at[r, pl.ds(0, 15)], mid_send.at[r])
        all_copied(gath.at[r, pl.ds(0, 31)], gath_send.at[r])
    all_copied(tiny_col.at[pl.ds(0, 15)], tiny_send.at[0])
    all_copied(tiny_hist.at[pl.ds(0, 31)], tiny_send.at[1])
    all_copied(cols0.at[:, :, :, pl.ds(0, 15)], in_send)
    all_copied(cols3.at[:, :, :, 0], local_sem)
    all_copied(row_back, back_sem)
    all_copied(cols3.at[:, :, :, pl.ds(0, 15)], out_send)
    for a in (0, 1):
        all_copied(cols3.at[a, :, :, pl.ds(0, 15)], out_recv.at[a])


def per_device(less_row, less_col, great_row, great_col, density, hamiltonian):
    history = jax.ShapeDtypeStruct(less_row.shape, BF)
    planes = pltpu.VMEM((2, 2, 8, 16, 8, NORB), BF)
    dma = pltpu.SemaphoreType.DMA
    hbm = pl.BlockSpec(memory_space=pltpu.HBM)
    vmem = pl.BlockSpec(memory_space=pltpu.VMEM)
    *fast, residual = pl.pallas_call(
        kernel,
        out_shape=(history,) * 4
        + (
            jax.ShapeDtypeStruct(density.shape, F32),
            jax.ShapeDtypeStruct((8, NORB), F32),
        ),
        in_specs=[hbm] * 4 + [vmem] * 2,
        out_specs=(hbm,) * 4 + (vmem,) * 2,
        scratch_shapes=[
            pltpu.VMEM((2, *less_row.shape), BF),
            *[planes] * 8,
            pltpu.VMEM((2, *less_row.shape), BF),
            pltpu.VMEM((2, 32, 8, NORB), F32),
            pltpu.VMEM((2, 32, 8, NORB), F32),
            pltpu.VMEM((2, 16, 8, NORB), F32),
            pltpu.VMEM((2, 32, 8, NORB), F32),
            pltpu.VMEM((16, 1, NORB), F32),
            pltpu.VMEM((32, 1, NORB), F32),
            dma, dma((16,)), dma, dma, dma, dma((2,)), dma,
            *[dma((2,))] * 8,
        ],
        compiler_params=pltpu.CompilerParams(
            collective_id=0, has_side_effects=True, vmem_limit_bytes=48 * 2**20
        ),
        cost_estimate=pl.CostEstimate(flops=4 * 10**9, bytes_accessed=8 * 2**20, transcendentals=0),
    )(less_row, less_col, great_row, great_col, density, hamiltonian)
    return lax.cond(
        residual[0, 0] < RESIDUAL_MAX,
        lambda done, given: done,
        lambda done, given: direct_steps(*given),
        tuple(fast),
        (less_row, less_col, great_row, great_col, density, hamiltonian),
    )


def solution(mesh):
    in_specs = (
        P(None, None, "col", "hist"),
        P(None, None, "col", "hist"),
        P(None, None, "col", "hist"),
        P(None, None, "col", "hist"),
        P(),
        P(),
    )
    out_specs = (
        P(None, None, "col", "hist"),
        P(None, None, "col", "hist"),
        P(None, None, "col", "hist"),
        P(None, None, "col", "hist"),
        P(),
    )
    return jax.shard_map(
        per_device, mesh=mesh, in_specs=in_specs, out_specs=out_specs, check_vma=False
    )
```

profile of v0, /device:TPU:1, one launch (start us, length us, event | category | flops | bytes accessed | tf_op | source)
XLA Modules:
  0.0 109.2 jit_solution(17254702249136870699)
XLA Ops:
  0.6 0.0 copy-start.16
  0.6 0.0 copy-start.21
  0.7 0.0 copy-start.17
  0.7 0.0 copy-start.22
  0.7 0.0 copy-start.23
  0.7 101.2 %shard_map.111 = (bf16[2,128,8,128]{3,2,1,0:T(8,128)(2,1)}, bf16[2,128,8,128]{3,2,1,0:T(8,128)(2,1)}, bf16[2,128,8,128]{3,2,1,0:T(8,128)(2,1)}, bf16[2,128,8,128...) custom-call(bf16[2,128,8,128]{3,2,1,0:T(8,128)(2,1)} %less_row.1, ...), custom_call_target="tpu_custom_call" | custom-call | flops 4000000000 | bytes 8388608 | tf_op jit(solution)/shard_map/pallas_call | solution.py:535
  101.9 0.5 slice.112
  103.1 0.0 copy-done.16
  103.1 0.0 copy-done.21
  103.1 0.0 copy-done.17
  103.1 0.0 copy-done.22
  103.1 0.0 copy-done.23
  103.1 0.2 conditional.1
  103.4 0.0 copy-start.18
  103.4 1.9 %copy.399 = bf16[2,128,8,128]{3,2,1,0:T(8,128)(2,1)} copy(bf16[2,128,8,128]{3,2,1,0:T(8,128)(2,1)} %get-tuple-element.193) | data formatting | bytes 1048576
  105.3 0.0 copy-done.18
  105.3 0.0 copy-start.20
  105.3 0.8 copy.400
  106.1 0.4 copy-done.20
  106.6 0.0 copy-start.19
  106.6 0.8 copy.401
  107.3 0.4 copy-done.19
  107.8 0.8 copy.402
  108.6 0.7 copy.403
Async XLA Ops:
  0.6 102.5 %copy-start.16 = (bf16[2,128,8,128]{3,2,1,0:T(8,128)(2,1)S(1)}, bf16[2,128,8,128]{3,2,1,0:T(8,128)(2,1)}, u32[]{:S(2)}) copy-start(bf16[2,128,8,128]{3,2,1,0:T(8,128)(2,1)} %less_row.1) | copy-start | bytes 1572868
  0.6 102.5 %copy-start.21 = (bf16[2,128,8,128]{3,2,1,0:T(8,128)(2,1)S(1)}, bf16[2,128,8,128]{3,2,1,0:T(8,128)(2,1)}, u32[]{:S(2)}) copy-start(bf16[2,128,8,128]{3,2,1,0:T(8,128)(2,1)} %less_col.1) | copy-start | bytes 1572868
  0.7 102.5 %copy-start.17 = (bf16[2,128,8,128]{3,2,1,0:T(8,128)(2,1)S(1)}, bf16[2,128,8,128]{3,2,1,0:T(8,128)(2,1)}, u32[]{:S(2)}) copy-start(bf16[2,128,8,128]{3,2,1,0:T(8,128)(2,1)} %great_row.1) | copy-start | bytes 1572868
  0.7 102.5 %copy-start.22 = (bf16[2,128,8,128]{3,2,1,0:T(8,128)(2,1)S(1)}, bf16[2,128,8,128]{3,2,1,0:T(8,128)(2,1)}, u32[]{:S(2)}) copy-start(bf16[2,128,8,128]{3,2,1,0:T(8,128)(2,1)} %great_col.1) | copy-start | bytes 1572868
  0.7 102.5 %copy-start.23 = (f32[128,128]{1,0:T(8,128)S(1)}, f32[128,128]{1,0:T(8,128)}, u32[]{:S(2)}) copy-start(f32[128,128]{1,0:T(8,128)} %ham_ref.1) | copy-start | bytes 196612
  103.4 1.9 %copy-start.18 = (bf16[2,128,8,128]{3,2,1,0:T(8,128)(2,1)S(1)}, bf16[2,128,8,128]{3,2,1,0:T(8,128)(2,1)}, u32[]{:S(2)}) copy-start(bf16[2,128,8,128]{3,2,1,0:T(8,128)(2,1)} %get-tuple-element.194) | copy-start | bytes 1572868
  105.3 1.2 %copy-start.20 = (bf16[2,128,8,128]{3,2,1,0:T(8,128)(2,1)S(1)}, bf16[2,128,8,128]{3,2,1,0:T(8,128)(2,1)}, u32[]{:S(2)}) copy-start(bf16[2,128,8,128]{3,2,1,0:T(8,128)(2,1)} %get-tuple-element.195) | copy-start | bytes 1572868
  106.6 1.2 %copy-start.19 = (bf16[2,128,8,128]{3,2,1,0:T(8,128)(2,1)S(1)}, bf16[2,128,8,128]{3,2,1,0:T(8,128)(2,1)}, u32[]{:S(2)}) copy-start(bf16[2,128,8,128]{3,2,1,0:T(8,128)(2,1)} %get-tuple-element.196) | copy-start | bytes 1572868
where the time goes:
time: 110 us; the launch traced here: 109 us
  Pallas kernels  101 us (92%)
  local copies, waits for them, and re-layouts  6.37 us (6%)
  between operations  1.39 us (1%)
    pallas_call x1, Pallas kernels, per_device(): pl.pallas_call(kernel, out_shape=(history,) * 4 + (jax.ShapeDtypeStruct(d...  101 us
    unnamed x21, local copies, waits for them, and re-layouts  5.86 us

commit v1 on v0

--- a/solution.py
+++ b/solution.py
@@ -170,6 +170,7 @@
 MESH = pl.DeviceIdType.MESH
 COL_PEERS = [(dz, dc) for dz in (4, 3, 5, 2, 6, 1, 7) for dc in (0, 1)] + [(0, 1)]
 RESIDUAL_MAX = 3e-4
+EARLY = 3
 
 
 def split_terms(x):
@@ -259,7 +260,7 @@
     return jnp.concatenate(sides, axis=1)
 
 
-def advance(weights, src, dst):
+def advance(weights, src, dst, arrays=(0, 1)):
     def one(a, carry):
         for k in range(0, 8, 2):
             out = jnp.dot(weights, pair_of(src, a, k), preferred_element_type=F32).astype(BF)
@@ -269,7 +270,10 @@
                     dst[a, comp, k + side] = block.reshape(16, 8, NORB)
         return carry
 
-    lax.fori_loop(0, 2, one, 0)
+    if len(arrays) == 2:
+        lax.fori_loop(0, 2, one, 0)
+    else:
+        one(arrays[0], 0)
 
 
 def self_energy_block(rows, cols, sigma, a, block):
@@ -314,10 +318,10 @@
 def kernel(
     less_row, less_col, great_row, great_col, rho_ref, ham_ref,
     less_row_out, less_col_out, great_row_out, great_col_out, rho_out, residual_out,
-    row_in, rows0, rows1, rows2, cols0, cols1, cols2, cols3, sigma, row_back,
-    scat_src, scat, mid, gath, tiny_col, tiny_hist,
-    in_send, in_recv, local_sem, row_sem, out_send, out_recv, back_sem,
-    scat_send, scat_recv, mid_send, mid_recv, gath_send, gath_recv, tiny_send, tiny_recv,
+    row_in, col_in, rows0, rows1, rows2, cols0, cols1, cols2, cols3, sigma, row_back,
+    scat_src0, scat0, mid0, gath0, scat_src1, scat1, mid1, gath1, tiny_col, tiny_hist,
+    in_send, in_recv, local_sem, row_sem, col_sem, out_send, out_recv, back_sem,
+    sum_send, sum_recv,
 ):
     me_col, me_hist = lax.axis_index("col"), lax.axis_index("hist")
     me_z, me_core = me_col // 2, lax.rem(me_col, 2)
@@ -338,6 +342,7 @@
             device_id={axis: peer}, device_id_type=MESH,
         ).start()
 
+    drains = []
     barrier = pltpu.get_barrier_semaphore()
     for dz, dc in COL_PEERS:
         pl.semaphore_signal(
@@ -348,9 +353,13 @@
     )
     row_refs, col_refs = (great_row, less_row), (less_col, great_col)
     for a in (0, 1):
+        pltpu.make_async_copy(col_refs[a], col_in.at[a], col_sem).start()
+    for a in (0, 1):
         pltpu.make_async_copy(row_refs[a], row_in.at[a], row_sem).start()
+    all_copied(col_in, col_sem)
+    for a in (0, 1):
         pltpu.make_async_copy(
-            col_refs[a].at[:, pl.ds(me_col * 8, 8)], cols0.at[a, :, :, me_col], local_sem
+            col_in.at[a, :, pl.ds(me_col * 8, 8)], cols0.at[a, :, :, me_col], local_sem
         ).start()
     pl.semaphore_wait(barrier, 46)
 
@@ -358,9 +367,10 @@
         peer = col_peer(dz, dc)
         for a in (0, 1):
             push(
-                col_refs[a].at[:, pl.ds(peer * 8, 8)], cols0.at[a, :, :, me_col],
+                col_in.at[a, :, pl.ds(peer * 8, 8)], cols0.at[a, :, :, me_col],
                 in_send, in_recv.at[me_col], "col", peer,
             )
+    drains.append(lambda: all_copied(cols0.at[:, :, :, pl.ds(0, 15)], in_send))
 
     eye_at = lax.broadcasted_iota(jnp.int32, (NORB, NORB), 0) == lax.broadcasted_iota(
         jnp.int32, (NORB, NORB), 1
@@ -405,93 +415,96 @@
         for a in (0, 1):
             self_energy_block(rows0, cols0, sigma, a, peer)
 
-    def scatter_sum(r, matrix):
-        for comp in (0, 1):
-            scat_src[r, pl.ds(16 * comp, 16)] = matrix[comp].reshape(16, 8, NORB)
-        hist_peers(
-            lambda p: push(
-                scat_src.at[r, p], scat.at[r, me_hist],
-                scat_send.at[r], scat_recv.at[r], "hist", p,
-            )
+    def scatter(source, target, send, recv):
+        hist_peers(lambda p: push(source.at[p], target.at[me_hist], send, recv, "hist", p))
+        target[me_hist] = source[me_hist]
+        drains.append(lambda: all_copied(source.at[pl.ds(0, 31)], send))
+
+    def give_all(buffer, value, send, recv, axis):
+        me, count = (me_col, 15) if axis == "col" else (me_hist, 31)
+        buffer[me] = value
+        if axis == "col":
+            for dz, dc in COL_PEERS:
+                push(buffer.at[me], buffer.at[me], send, recv, axis, col_peer(dz, dc))
+        else:
+            hist_peers(lambda p: push(buffer.at[me], buffer.at[me], send, recv, axis, p))
+        drains.append(lambda: all_copied(buffer.at[pl.ds(0, count)], send))
+
+    def arrived(buffer, recv):
+        all_copied(buffer.at[pl.ds(0, buffer.shape[0] - 1)], recv)
+
+    def whole(buffer, rows):
+        return tuple(
+            buffer[pl.ds(16 * comp, 16), rows : rows + 8].reshape(NORB, NORB) for comp in (0, 1)
         )
-        scat[r, me_hist] = scat_src[r, me_hist]
-
-    def middle_sum(r):
-        all_copied(scat.at[r, pl.ds(0, 31)], scat_recv.at[r])
-        mid[r, me_col] = jnp.sum(scat[r], axis=0)
-        for dz, dc in COL_PEERS:
-            push(
-                mid.at[r, me_col], mid.at[r, me_col],
-                mid_send.at[r], mid_recv.at[r], "col", col_peer(dz, dc),
-            )
-
-    def gather_sum(r):
-        all_copied(mid.at[r, pl.ds(0, 15)], mid_recv.at[r])
-        gath[r, me_hist] = jnp.sum(mid[r], axis=0)
-        hist_peers(
-            lambda p: push(
-                gath.at[r, me_hist], gath.at[r, me_hist],
-                gath_send.at[r], gath_recv.at[r], "hist", p,
-            )
-        )
-
-    def summed(r):
-        all_copied(gath.at[r, pl.ds(0, 31)], gath_recv.at[r])
-        return tuple(gath[r, pl.ds(16 * comp, 16)].reshape(NORB, NORB) for comp in (0, 1))
-
-    scatter_sum(0, collision_of(sigma, cols0))
+
+    first = collision_of(sigma, cols0)
+    give_all(tiny_col, diagonals(first[0])[0], sum_send.at[1], sum_recv.at[1], "col")
+    for comp in (0, 1):
+        scat_src0[pl.ds(16 * comp, 16)] = first[comp].reshape(16, 8, NORB).astype(BF)
+    scatter(scat_src0, scat0, sum_send.at[0], sum_recv.at[0])
     advance(weight_cols1, cols0, cols1)
     self_energy_all(rows1, cols1, sigma)
     second = collision_of(sigma, cols1)
-    middle_sum(0)
-    tiny_col[me_col] = jnp.sum(jnp.where(eye_at, second[0], 0.0), axis=0, keepdims=True)
-    for dz, dc in COL_PEERS:
-        push(
-            tiny_col.at[me_col], tiny_col.at[me_col],
-            tiny_send.at[0], tiny_recv.at[0], "col", col_peer(dz, dc),
-        )
-    gather_sum(0)
-    all_copied(tiny_col.at[pl.ds(0, 15)], tiny_recv.at[0])
-    tiny_hist[me_hist] = jnp.sum(tiny_col[...], axis=0)
-    hist_peers(
-        lambda p: push(
-            tiny_hist.at[me_hist], tiny_hist.at[me_hist],
-            tiny_send.at[1], tiny_recv.at[1], "hist", p,
-        )
-    )
-    first = summed(0)
-
-    density1 = (rotated1[0] + first[0], rotated1[1] + first[1])
-    unit2, diag2 = unitary_of(density1[0])
+    for comp in (0, 1):
+        scat_src1[pl.ds(16 * comp, 16), 0:8] = second[comp].reshape(16, 8, NORB).astype(BF)
+    second_diag = jnp.broadcast_to(diagonals(second[0])[0], (8, NORB))
+    arrived(scat0, sum_recv.at[0])
+    piece = jnp.sum(scat0[...].astype(F32), axis=0)
+    give_all(
+        mid0, jnp.concatenate([piece, second_diag], axis=0), sum_send.at[2], sum_recv.at[2], "col"
+    )
+    arrived(tiny_col, sum_recv.at[1])
+    give_all(
+        tiny_hist, jnp.sum(tiny_col[...], axis=0), sum_send.at[3], sum_recv.at[3], "hist"
+    )
+    arrived(mid0, sum_recv.at[2])
+    give_all(gath0, jnp.sum(mid0[...], axis=0), sum_send.at[4], sum_recv.at[4], "hist")
+    arrived(tiny_hist, sum_recv.at[3])
+    first_diag = jnp.sum(tiny_hist[...], axis=0)
+    unit2, diag2 = unitary_of(rotated1[0] + jnp.where(eye_at, first_diag, 0.0))
     weight_rows2, weight_cols2 = stacked_low(unit2, 1.0), stacked_low(unit2, -1.0)
-    rotated2 = rotate(unit2, density1)
-    all_copied(tiny_hist.at[pl.ds(0, 31)], tiny_recv.at[1])
-    second_diag = jnp.sum(tiny_hist[...], axis=0)
+    advance(weight_cols2, cols1, cols2)
+    advance(weight_rows2, rows1, rows2)
+    self_energy_all(rows2, cols2, sigma)
+    third = collision_of(sigma, cols2)
+    for comp in (0, 1):
+        scat_src1[pl.ds(16 * comp, 16), 8:16] = third[comp].reshape(16, 8, NORB).astype(BF)
+    scatter(scat_src1, scat1, sum_send.at[5], sum_recv.at[5])
+
+    arrived(gath0, sum_recv.at[4])
+    first = whole(gath0, 0)
+    second_diag = jnp.sum(gath0[:, 8:16], axis=0)[0:1]
+    rotated2 = rotate(unit2, (rotated1[0] + first[0], rotated1[1] + first[1]))
     unit3, diag3 = unitary_of(rotated2[0] + jnp.where(eye_at, second_diag, 0.0))
     weight_rows3, weight_cols3 = stacked_low(unit3, 1.0), stacked_low(unit3, -1.0)
 
-    advance(weight_cols2, cols1, cols2)
-    advance(weight_cols3, cols2, cols3)
     col_outs, row_outs = (less_col_out, great_col_out), (great_row_out, less_row_out)
-    for dz, dc in COL_PEERS:
-        peer = col_peer(dz, dc)
-        for a in (0, 1):
+    returns = [(a, dz, dc) for a in (0, 1) for dz, dc in COL_PEERS]
+
+    def give_back(some):
+        for a, dz, dc in some:
             push(
-                cols3.at[a, :, :, peer], col_outs[a].at[:, pl.ds(me_col * 8, 8)],
-                out_send, out_recv.at[a], "col", peer,
+                cols3.at[a, :, :, col_peer(dz, dc)], col_outs[a].at[:, pl.ds(me_col * 8, 8)],
+                out_send, out_recv.at[a], "col", col_peer(dz, dc),
             )
+
+    advance(weight_cols3, cols2, cols3, (0,))
+    give_back(returns[:EARLY])
+    advance(weight_cols3, cols2, cols3, (1,))
     for a in (0, 1):
         pltpu.make_async_copy(
             cols3.at[a, :, :, me_col], col_outs[a].at[:, pl.ds(me_col * 8, 8)], local_sem
         ).start()
-
-    advance(weight_rows2, rows1, rows2)
-    self_energy_all(rows2, cols2, sigma)
-    third = collision_of(sigma, cols2)
-    turned = rotate(unit3, second)
-    scatter_sum(1, (turned[0] + third[0], turned[1] + third[1]))
+        drains.append(lambda a=a: all_copied(cols3.at[a, :, :, pl.ds(0, 15)], out_recv.at[a]))
+    drains.append(lambda: all_copied(cols3.at[:, :, :, 0], local_sem))
+    drains.append(lambda: all_copied(cols3.at[:, :, :, pl.ds(0, 15)], out_send))
+
+    arrived(scat1, sum_recv.at[5])
+    pieces = jnp.sum(scat1[...].astype(F32), axis=0)
+    give_all(mid1, pieces.astype(BF), sum_send.at[6], sum_recv.at[6], "col")
+    give_back(returns[EARLY:])
     advance(weight_rows3, rows2, rows0)
-    middle_sum(1)
 
     def turn_out(block, carry):
         for a in (0, 1):
@@ -503,27 +516,35 @@
     lax.fori_loop(0, 16, turn_out, 0)
     for a in (0, 1):
         pltpu.make_async_copy(row_back.at[a], row_outs[a], back_sem).start()
-    gather_sum(1)
+    drains.append(lambda: all_copied(row_back, back_sem))
+    arrived(mid1, sum_recv.at[6])
+    pieces = jnp.sum(mid1[...].astype(F32), axis=0)
+    give_all(gath1, pieces, sum_send.at[7], sum_recv.at[7], "hist")
     residual = jnp.maximum(residual, residual_of(eye, off, diag2, unit2))
     residual = jnp.maximum(residual, residual_of(eye, off, diag3, unit3))
-    residual_out[...] = jnp.broadcast_to(residual, (8, NORB))
-    rotated3 = rotate(unit3, rotated2)
-    last = summed(1)
+    residual_out[...] = residual
+    arrived(gath1, sum_recv.at[7])
+    second, third = whole(gath1, 0), whole(gath1, 8)
+    rotated3 = rotate(unit3, (rotated2[0] + second[0], rotated2[1] + second[1]))
     for comp in (0, 1):
-        rho_out[comp] = rotated3[comp] + last[comp]
-
-    for r in (0, 1):
-        all_copied(scat_src.at[r, pl.ds(0, 31)], scat_send.at[r])
-        all_copied(mid.at[r, pl.ds(0, 15)], mid_send.at[r])
-        all_copied(gath.at[r, pl.ds(0, 31)], gath_send.at[r])
-    all_copied(tiny_col.at[pl.ds(0, 15)], tiny_send.at[0])
-    all_copied(tiny_hist.at[pl.ds(0, 31)], tiny_send.at[1])
-    all_copied(cols0.at[:, :, :, pl.ds(0, 15)], in_send)
-    all_copied(cols3.at[:, :, :, 0], local_sem)
-    all_copied(row_back, back_sem)
-    all_copied(cols3.at[:, :, :, pl.ds(0, 15)], out_send)
-    for a in (0, 1):
-        all_copied(cols3.at[a, :, :, pl.ds(0, 15)], out_recv.at[a])
+        rho_out[comp] = rotated3[comp] + third[comp]
+
+    for drain in drains:
+        drain()
+
+
+def unload(*refs):
+    sources, targets, stops = refs[:5], refs[5:10], refs[10:15]
+    in_sem, out_sem = refs[15:]
+    ins = [pltpu.make_async_copy(sources[n], stops[n], in_sem.at[n]) for n in range(5)]
+    outs = [pltpu.make_async_copy(stops[n], targets[n], out_sem.at[n]) for n in range(5)]
+    for copy in ins:
+        copy.start()
+    for n in range(5):
+        ins[n].wait()
+        outs[n].start()
+    for copy in outs:
+        copy.wait()
 
 
 def per_device(less_row, less_col, great_row, great_col, density, hamiltonian):
@@ -537,31 +558,47 @@
         out_shape=(history,) * 4
         + (
             jax.ShapeDtypeStruct(density.shape, F32),
-            jax.ShapeDtypeStruct((8, NORB), F32),
+            jax.ShapeDtypeStruct((1, 1), F32),
         ),
         in_specs=[hbm] * 4 + [vmem] * 2,
         out_specs=(hbm,) * 4 + (vmem,) * 2,
         scratch_shapes=[
-            pltpu.VMEM((2, *less_row.shape), BF),
+            *[pltpu.VMEM((2, *less_row.shape), BF)] * 2,
             *[planes] * 8,
             pltpu.VMEM((2, *less_row.shape), BF),
-            pltpu.VMEM((2, 32, 8, NORB), F32),
-            pltpu.VMEM((2, 32, 8, NORB), F32),
-            pltpu.VMEM((2, 16, 8, NORB), F32),
-            pltpu.VMEM((2, 32, 8, NORB), F32),
+            pltpu.VMEM((32, 8, NORB), BF),
+            pltpu.VMEM((32, 8, NORB), BF),
+            pltpu.VMEM((16, 16, NORB), F32),
+            pltpu.VMEM((32, 16, NORB), F32),
+            pltpu.VMEM((32, 16, NORB), BF),
+            pltpu.VMEM((32, 16, NORB), BF),
+            pltpu.VMEM((16, 16, NORB), BF),
+            pltpu.VMEM((32, 16, NORB), F32),
             pltpu.VMEM((16, 1, NORB), F32),
             pltpu.VMEM((32, 1, NORB), F32),
-            dma, dma((16,)), dma, dma, dma, dma((2,)), dma,
-            *[dma((2,))] * 8,
+            dma, dma((16,)), dma, dma, dma, dma, dma((2,)), dma,
+            dma((8,)), dma((8,)),
         ],
         compiler_params=pltpu.CompilerParams(
-            collective_id=0, has_side_effects=True, vmem_limit_bytes=48 * 2**20
+            collective_id=0, has_side_effects=True, vmem_limit_bytes=24 * 2**20
         ),
         cost_estimate=pl.CostEstimate(flops=4 * 10**9, bytes_accessed=8 * 2**20, transcendentals=0),
     )(less_row, less_col, great_row, great_col, density, hamiltonian)
+    place = pl.pallas_call(
+        unload,
+        out_shape=tuple(jax.ShapeDtypeStruct(x.shape, x.dtype) for x in fast),
+        in_specs=[hbm] * 5,
+        out_specs=(hbm,) * 5,
+        scratch_shapes=[
+            *[pltpu.VMEM(x.shape, x.dtype) for x in fast],
+            dma((5,)),
+            dma((5,)),
+        ],
+        compiler_params=pltpu.CompilerParams(vmem_limit_bytes=60 * 2**20),
+    )
     return lax.cond(
         residual[0, 0] < RESIDUAL_MAX,
-        lambda done, given: done,
+        lambda done, given: tuple(place(*done)),
         lambda done, given: direct_steps(*given),
         tuple(fast),
         (less_row, less_col, great_row, great_col, density, hamiltonian),

time: 110 us -> 97.4 us (0.89)
  local copies, waits for them, and re-layouts: 6.37 us -> 0.02 us
  Pallas kernels: 101 us -> 95.5 us
    pallas_call x1, Pallas kernels: 101 us -> 93 us  [per_device(): pl.pallas_call(kernel, out_shape=(history,) * 4 + (jax.ShapeDtypeStruct(d...]
    unnamed x21 -> x10, local copies, waits for them, and re-layouts: 5.86 us -> 0.02 us
    pallas_call x0 -> x1, Pallas kernels: none -> 2.47 us  [per_device(): place(*done)]
where the time goes in v1:
time: 97.4 us; the launch traced here: 97.2 us
  Pallas kernels  95.5 us (98%)
  between operations  1.44 us (1%)
    pallas_call x1, Pallas kernels, per_device(): pl.pallas_call(kernel, out_shape=(history,) * 4 + (jax.ShapeDtypeStruct(d...  93 us
    pallas_call x1, Pallas kernels, per_device(): place(*done)  2.47 us

profile of v1, /device:TPU:1, one launch (start us, length us, event | category | flops | bytes accessed | tf_op | source)
XLA Modules:
  0.0 97.2 jit_solution(16690541844027717900)
XLA Ops:
  0.6 0.0 copy-start.16
  0.6 0.0 copy-start.18
  0.7 0.0 copy-start.17
  0.7 0.0 copy-start.19
  0.7 0.0 copy-start.20
  0.7 93.0 %shard_map.111 = (bf16[2,128,8,128]{3,2,1,0:T(8,128)(2,1)}, bf16[2,128,8,128]{3,2,1,0:T(8,128)(2,1)}, bf16[2,128,8,128]{3,2,1,0:T(8,128)(2,1)}, bf16[2,128,8,128...) custom-call(bf16[2,128,8,128]{3,2,1,0:T(8,128)(2,1)} %less_row.1, bf16[2,128,8,128]{3,2,1,0:T(8,128)(2,1)} %less_col.1, ...), custom_call_target="tpu_custom_call" | custom-call | flops 4000000000 | bytes 8388608 | tf_op jit(solution)/shard_map/pallas_call | solution.py:556
  94.3 0.0 copy-done.16
  94.3 0.0 copy-done.18
  94.3 0.0 copy-done.17
  94.3 0.0 copy-done.19
  94.3 0.0 copy-done.20
  94.3 2.7 %conditional.1 = ((bf16[2,128,8,128]{3,2,1,0:T(8,128)(2,1)}, bf16[2,128,8,128]{3,2,1,0:T(8,128)(2,1)}, bf16[2,128,8,128]{3,2,1,0:T(8,128)(2,1)}, bf16[2,128,8,128]{3,2,1,0:T(8,128)(2,1)}, f32[2,128,128]{2,1,0:T(8,128)})) conditional(s32[]{:T(128)} %bitcast.153, (f32[128,128]{1,0:T(8,128)S(1)}, f32[2,128,128]{2,1,0:T(8,128)}, ...), branch_computations={%region_0.11_spmd, %region_9.12_spmd} | conditional | flops 3422454784 | bytes 161379776 | solution.py:599
  94.6 2.5 %branch_1_fun.1 = (bf16[2,128,8,128]{3,2,1,0:T(8,128)(2,1)}, bf16[2,128,8,128]{3,2,1,0:T(8,128)(2,1)}, bf16[2,128,8,128]{3,2,1,0:T(8,128)(2,1)}, bf16[2,128,8,128]{3,2,1,0:T(8,128)(2,1)}, f32[2,128,128]{2,1,0:T(8,128)}) custom-call(bf16[2,128,8,128]{3,2,1,0:T(8,128)(2,1)} %get-tuple-element.30.refs_0_, bf16[2,128,8,128]{3,2,1,0:T(8,128)(2,1)} %get-tuple-element.31.refs_1_, ...), custom_call_target="tpu_custom_call" | custom-call | tf_op jit(solution)/shard_map/cond/branch_1_fun/pallas_call | solution.py:601
Async XLA Ops:
  0.6 93.6 %copy-start.16 = (bf16[2,128,8,128]{3,2,1,0:T(8,128)(2,1)S(1)}, bf16[2,128,8,128]{3,2,1,0:T(8,128)(2,1)}, u32[]{:S(2)}) copy-start(bf16[2,128,8,128]{3,2,1,0:T(8,128)(2,1)} %less_row.1) | copy-start | bytes 1572868
  0.6 93.6 %copy-start.18 = (bf16[2,128,8,128]{3,2,1,0:T(8,128)(2,1)S(1)}, bf16[2,128,8,128]{3,2,1,0:T(8,128)(2,1)}, u32[]{:S(2)}) copy-start(bf16[2,128,8,128]{3,2,1,0:T(8,128)(2,1)} %less_col.1) | copy-start | bytes 1572868
  0.7 93.6 %copy-start.17 = (bf16[2,128,8,128]{3,2,1,0:T(8,128)(2,1)S(1)}, bf16[2,128,8,128]{3,2,1,0:T(8,128)(2,1)}, u32[]{:S(2)}) copy-start(bf16[2,128,8,128]{3,2,1,0:T(8,128)(2,1)} %great_row.1) | copy-start | bytes 1572868
  0.7 93.6 %copy-start.19 = (bf16[2,128,8,128]{3,2,1,0:T(8,128)(2,1)S(1)}, bf16[2,128,8,128]{3,2,1,0:T(8,128)(2,1)}, u32[]{:S(2)}) copy-start(bf16[2,128,8,128]{3,2,1,0:T(8,128)(2,1)} %great_col.1) | copy-start | bytes 1572868
  0.7 93.6 %copy-start.20 = (f32[128,128]{1,0:T(8,128)S(1)}, f32[128,128]{1,0:T(8,128)}, u32[]{:S(2)}) copy-start(f32[128,128]{1,0:T(8,128)} %ham_ref.1) | copy-start | bytes 196612

commit v2 on v1

--- a/solution.py
+++ b/solution.py
@@ -221,7 +221,7 @@
     power = (inv_im_col * off, -inv_re_col * off)
     total = (eye + power[0], power[1])
     power = complex_dots([power], power)[0]
-    for last in (False, False, True):
+    for last in (False, True):
         if last:
             gain = complex_dots([total], power)[0]
         else:
@@ -435,7 +435,8 @@
 
     def whole(buffer, rows):
         return tuple(
-            buffer[pl.ds(16 * comp, 16), rows : rows + 8].reshape(NORB, NORB) for comp in (0, 1)
+            buffer[pl.ds(16 * comp, 16)].astype(F32)[:, rows : rows + 8].reshape(NORB, NORB)
+            for comp in (0, 1)
         )
 
     first = collision_of(sigma, cols0)
@@ -448,18 +449,29 @@
     second = collision_of(sigma, cols1)
     for comp in (0, 1):
         scat_src1[pl.ds(16 * comp, 16), 0:8] = second[comp].reshape(16, 8, NORB).astype(BF)
-    second_diag = jnp.broadcast_to(diagonals(second[0])[0], (8, NORB))
+    second_diag = diagonals(second[0])[0]
+    upper = lax.broadcasted_iota(jnp.int32, (8, NORB), 0) < 4
+
+    def with_diagonal(piece, diag):
+        high, low = split_terms(jnp.broadcast_to(diag, (8, NORB)))
+        tail = jnp.where(upper, high.astype(F32), low.astype(F32))
+        return jnp.concatenate([piece, tail], axis=0).astype(BF)
+
+    def diagonal_in(total):
+        return total[8:9] + total[12:13]
+
     arrived(scat0, sum_recv.at[0])
     piece = jnp.sum(scat0[...].astype(F32), axis=0)
-    give_all(
-        mid0, jnp.concatenate([piece, second_diag], axis=0), sum_send.at[2], sum_recv.at[2], "col"
-    )
+    give_all(mid0, with_diagonal(piece, second_diag), sum_send.at[2], sum_recv.at[2], "col")
     arrived(tiny_col, sum_recv.at[1])
     give_all(
         tiny_hist, jnp.sum(tiny_col[...], axis=0), sum_send.at[3], sum_recv.at[3], "hist"
     )
     arrived(mid0, sum_recv.at[2])
-    give_all(gath0, jnp.sum(mid0[...], axis=0), sum_send.at[4], sum_recv.at[4], "hist")
+    total = jnp.sum(mid0[...].astype(F32), axis=0)
+    give_all(
+        gath0, with_diagonal(total[0:8], diagonal_in(total)), sum_send.at[4], sum_recv.at[4], "hist"
+    )
     arrived(tiny_hist, sum_recv.at[3])
     first_diag = jnp.sum(tiny_hist[...], axis=0)
     unit2, diag2 = unitary_of(rotated1[0] + jnp.where(eye_at, first_diag, 0.0))
@@ -474,7 +486,7 @@
 
     arrived(gath0, sum_recv.at[4])
     first = whole(gath0, 0)
-    second_diag = jnp.sum(gath0[:, 8:16], axis=0)[0:1]
+    second_diag = diagonal_in(jnp.sum(gath0[...].astype(F32), axis=0))
     rotated2 = rotate(unit2, (rotated1[0] + first[0], rotated1[1] + first[1]))
     unit3, diag3 = unitary_of(rotated2[0] + jnp.where(eye_at, second_diag, 0.0))
     weight_rows3, weight_cols3 = stacked_low(unit3, 1.0), stacked_low(unit3, -1.0)
@@ -568,8 +580,8 @@
             pltpu.VMEM((2, *less_row.shape), BF),
             pltpu.VMEM((32, 8, NORB), BF),
             pltpu.VMEM((32, 8, NORB), BF),
-            pltpu.VMEM((16, 16, NORB), F32),
-            pltpu.VMEM((32, 16, NORB), F32),
+            pltpu.VMEM((16, 16, NORB), BF),
+            pltpu.VMEM((32, 16, NORB), BF),
             pltpu.VMEM((32, 16, NORB), BF),
             pltpu.VMEM((32, 16, NORB), BF),
             pltpu.VMEM((16, 16, NORB), BF),

time: 97.4 us -> 94.3 us (0.968)
  Pallas kernels: 95.5 us -> 92.4 us
    pallas_call x1, Pallas kernels: 93 us -> 89.9 us  [per_device(): pl.pallas_call(kernel, out_shape=(history,) * 4 + (jax.ShapeDtypeStruct(d...]
where the time goes in v2:
time: 94.3 us; the launch traced here: 94.1 us
  Pallas kernels  92.4 us (98%)
  between operations  1.44 us (2%)
    pallas_call x1, Pallas kernels, per_device(): pl.pallas_call(kernel, out_shape=(history,) * 4 + (jax.ShapeDtypeStruct(d...  89.9 us
    pallas_call x1, Pallas kernels, per_device(): place(*done)  2.47 us

profile of v2, /device:TPU:1, one launch (start us, length us, event | category | flops | bytes accessed | tf_op | source)
XLA Modules:
  0.0 94.1 jit_solution(1555228358330795407)
XLA Ops:
  0.6 0.0 copy-start.16
  0.6 0.0 copy-start.18
  0.7 0.0 copy-start.17
  0.7 0.0 copy-start.19
  0.7 0.0 copy-start.20
  0.7 89.9 %shard_map.111 = (bf16[2,128,8,128]{3,2,1,0:T(8,128)(2,1)}, bf16[2,128,8,128]{3,2,1,0:T(8,128)(2,1)}, bf16[2,128,8,128]{3,2,1,0:T(8,128)(2,1)}, bf16[2,128,8,128...) custom-call(bf16[2,128,8,128]{3,2,1,0:T(8,128)(2,1)} %less_row.1, bf16[2,128,8,128]{3,2,1,0:T(8,128)(2,1)} %less_col.1, ...), custom_call_target="tpu_custom_call" | custom-call | flops 4000000000 | bytes 8388608 | tf_op jit(solution)/shard_map/pallas_call | solution.py:568
  91.1 0.0 copy-done.16
  91.2 0.0 copy-done.18
  91.2 0.0 copy-done.17
  91.2 0.0 copy-done.19
  91.2 0.0 copy-done.20
  91.2 2.7 %conditional.1 = ((bf16[2,128,8,128]{3,2,1,0:T(8,128)(2,1)}, bf16[2,128,8,128]{3,2,1,0:T(8,128)(2,1)}, bf16[2,128,8,128]{3,2,1,0:T(8,128)(2,1)}, bf16[2,128,8,128]{3,2,1,0:T(8,128)(2,1)}, f32[2,128,128]{2,1,0:T(8,128)})) conditional(s32[]{:T(128)} %bitcast.153, (f32[128,128]{1,0:T(8,128)S(1)}, f32[2,128,128]{2,1,0:T(8,128)}, ...), branch_computations={%region_0.11_spmd, %region_9.12_spmd} | conditional | flops 3422454784 | bytes 161379776 | solution.py:611
  91.4 2.5 %branch_1_fun.1 = (bf16[2,128,8,128]{3,2,1,0:T(8,128)(2,1)}, bf16[2,128,8,128]{3,2,1,0:T(8,128)(2,1)}, bf16[2,128,8,128]{3,2,1,0:T(8,128)(2,1)}, bf16[2,128,8,128]{3,2,1,0:T(8,128)(2,1)}, f32[2,128,128]{2,1,0:T(8,128)}) custom-call(bf16[2,128,8,128]{3,2,1,0:T(8,128)(2,1)} %get-tuple-element.30.refs_0_, bf16[2,128,8,128]{3,2,1,0:T(8,128)(2,1)} %get-tuple-element.31.refs_1_, ...), custom_call_target="tpu_custom_call" | custom-call | tf_op jit(solution)/shard_map/cond/branch_1_fun/pallas_call | solution.py:613
Async XLA Ops:
  0.6 90.5 %copy-start.16 = (bf16[2,128,8,128]{3,2,1,0:T(8,128)(2,1)S(1)}, bf16[2,128,8,128]{3,2,1,0:T(8,128)(2,1)}, u32[]{:S(2)}) copy-start(bf16[2,128,8,128]{3,2,1,0:T(8,128)(2,1)} %less_row.1) | copy-start | bytes 1572868
  0.6 90.5 %copy-start.18 = (bf16[2,128,8,128]{3,2,1,0:T(8,128)(2,1)S(1)}, bf16[2,128,8,128]{3,2,1,0:T(8,128)(2,1)}, u32[]{:S(2)}) copy-start(bf16[2,128,8,128]{3,2,1,0:T(8,128)(2,1)} %less_col.1) | copy-start | bytes 1572868
  0.7 90.5 %copy-start.17 = (bf16[2,128,8,128]{3,2,1,0:T(8,128)(2,1)S(1)}, bf16[2,128,8,128]{3,2,1,0:T(8,128)(2,1)}, u32[]{:S(2)}) copy-start(bf16[2,128,8,128]{3,2,1,0:T(8,128)(2,1)} %great_row.1) | copy-start | bytes 1572868
  0.7 90.5 %copy-start.19 = (bf16[2,128,8,128]{3,2,1,0:T(8,128)(2,1)S(1)}, bf16[2,128,8,128]{3,2,1,0:T(8,128)(2,1)}, u32[]{:S(2)}) copy-start(bf16[2,128,8,128]{3,2,1,0:T(8,128)(2,1)} %great_col.1) | copy-start | bytes 1572868
  0.7 90.5 %copy-start.20 = (f32[128,128]{1,0:T(8,128)S(1)}, f32[128,128]{1,0:T(8,128)}, u32[]{:S(2)}) copy-start(f32[128,128]{1,0:T(8,128)} %ham_ref.1) | copy-start | bytes 196612

commit v3 on v2

--- a/solution.py
+++ b/solution.py
@@ -170,7 +170,7 @@
 MESH = pl.DeviceIdType.MESH
 COL_PEERS = [(dz, dc) for dz in (4, 3, 5, 2, 6, 1, 7) for dc in (0, 1)] + [(0, 1)]
 RESIDUAL_MAX = 3e-4
-EARLY = 3
+EARLY = 6
 
 
 def split_terms(x):
@@ -207,7 +207,10 @@
 
 
 def rotate(unit, rho):
-    left = complex_dots([unit], rho)[0]
+    return rotate_right(complex_dots([unit], rho)[0], unit)
+
+
+def rotate_right(left, unit):
     product = fine_dot(jnp.concatenate(left, axis=0), jnp.concatenate(unit, axis=1))
     rr, ri, ir, ii = parts_of(product, 0)
     return rr + ii, ir - ri
@@ -482,13 +485,13 @@
     third = collision_of(sigma, cols2)
     for comp in (0, 1):
         scat_src1[pl.ds(16 * comp, 16), 8:16] = third[comp].reshape(16, 8, NORB).astype(BF)
-    scatter(scat_src1, scat1, sum_send.at[5], sum_recv.at[5])
 
     arrived(gath0, sum_recv.at[4])
     first = whole(gath0, 0)
     second_diag = diagonal_in(jnp.sum(gath0[...].astype(F32), axis=0))
-    rotated2 = rotate(unit2, (rotated1[0] + first[0], rotated1[1] + first[1]))
-    unit3, diag3 = unitary_of(rotated2[0] + jnp.where(eye_at, second_diag, 0.0))
+    left2 = complex_dots([unit2], (rotated1[0] + first[0], rotated1[1] + first[1]))[0]
+    turned_diag = jnp.sum(left2[0] * unit2[0] + left2[1] * unit2[1], axis=1, keepdims=True)
+    unit3, diag3 = unitary_of(jnp.where(eye_at, turned_diag + second_diag, 0.0))
     weight_rows3, weight_cols3 = stacked_low(unit3, 1.0), stacked_low(unit3, -1.0)
 
     col_outs, row_outs = (less_col_out, great_col_out), (great_row_out, less_row_out)
@@ -503,6 +506,7 @@
 
     advance(weight_cols3, cols2, cols3, (0,))
     give_back(returns[:EARLY])
+    scatter(scat_src1, scat1, sum_send.at[5], sum_recv.at[5])
     advance(weight_cols3, cols2, cols3, (1,))
     for a in (0, 1):
         pltpu.make_async_copy(
@@ -532,6 +536,7 @@
     arrived(mid1, sum_recv.at[6])
     pieces = jnp.sum(mid1[...].astype(F32), axis=0)
     give_all(gath1, pieces, sum_send.at[7], sum_recv.at[7], "hist")
+    rotated2 = rotate_right(left2, unit2)
     residual = jnp.maximum(residual, residual_of(eye, off, diag2, unit2))
     residual = jnp.maximum(residual, residual_of(eye, off, diag3, unit3))
     residual_out[...] = residual
@@ -546,34 +551,28 @@
 
 
 def unload(*refs):
-    sources, targets, stops = refs[:5], refs[5:10], refs[10:15]
-    in_sem, out_sem = refs[15:]
-    ins = [pltpu.make_async_copy(sources[n], stops[n], in_sem.at[n]) for n in range(5)]
-    outs = [pltpu.make_async_copy(stops[n], targets[n], out_sem.at[n]) for n in range(5)]
-    for copy in ins:
+    sources, targets, sem = refs[:5], refs[5:10], refs[10]
+    copies = [pltpu.make_async_copy(sources[n], targets[n], sem.at[n]) for n in range(5)]
+    for copy in copies:
         copy.start()
-    for n in range(5):
-        ins[n].wait()
-        outs[n].start()
-    for copy in outs:
+    for copy in copies:
         copy.wait()
 
 
 def per_device(less_row, less_col, great_row, great_col, density, hamiltonian):
-    history = jax.ShapeDtypeStruct(less_row.shape, BF)
     planes = pltpu.VMEM((2, 2, 8, 16, 8, NORB), BF)
     dma = pltpu.SemaphoreType.DMA
     hbm = pl.BlockSpec(memory_space=pltpu.HBM)
     vmem = pl.BlockSpec(memory_space=pltpu.VMEM)
     *fast, residual = pl.pallas_call(
         kernel,
-        out_shape=(history,) * 4
+        out_shape=(pltpu.VMEM(less_row.shape, BF),) * 4
         + (
-            jax.ShapeDtypeStruct(density.shape, F32),
+            pltpu.VMEM(density.shape, F32),
             jax.ShapeDtypeStruct((1, 1), F32),
         ),
         in_specs=[hbm] * 4 + [vmem] * 2,
-        out_specs=(hbm,) * 4 + (vmem,) * 2,
+        out_specs=(vmem,) * 6,
         scratch_shapes=[
             *[pltpu.VMEM((2, *less_row.shape), BF)] * 2,
             *[planes] * 8,
@@ -599,14 +598,10 @@
     place = pl.pallas_call(
         unload,
         out_shape=tuple(jax.ShapeDtypeStruct(x.shape, x.dtype) for x in fast),
-        in_specs=[hbm] * 5,
+        in_specs=[vmem] * 5,
         out_specs=(hbm,) * 5,
-        scratch_shapes=[
-            *[pltpu.VMEM(x.shape, x.dtype) for x in fast],
-            dma((5,)),
-            dma((5,)),
-        ],
-        compiler_params=pltpu.CompilerParams(vmem_limit_bytes=60 * 2**20),
+        scratch_shapes=[dma((5,))],
+        compiler_params=pltpu.CompilerParams(vmem_limit_bytes=4 * 2**20),
     )
     return lax.cond(
         residual[0, 0] < RESIDUAL_MAX,

time: 94.3 us -> 92.6 us (0.982)
  Pallas kernels: 92.4 us -> 90.6 us
    pallas_call x1, Pallas kernels: 2.47 us -> 1.39 us  [per_device(): place(*done)]
where the time goes in v3:
time: 92.6 us; the launch traced here: 92.4 us
  Pallas kernels  90.6 us (98%)
  between operations  1.56 us (2%)
    pallas_call x1, Pallas kernels, per_device(): pl.pallas_call(kernel, out_shape=(pltpu.VMEM(less_row.shape, BF),) * 4 +...  89.2 us

profile of v3, /device:TPU:1, one launch (start us, length us, event | category | flops | bytes accessed | tf_op | source)
XLA Modules:
  0.0 92.4 jit_solution(16220824204552866212)
XLA Ops:
  0.6 0.0 copy-start.18
  0.6 0.0 copy-start.17
  0.7 0.0 copy-start.19
  0.7 0.0 copy-start.20
  0.7 89.2 %shard_map.111 = (bf16[2,128,8,128]{3,2,1,0:T(8,128)(2,1)S(1)}, bf16[2,128,8,128]{3,2,1,0:T(8,128)(2,1)S(1)}, bf16[2,128,8,128]{3,2,1,0:T(8,128)(2,1)S(1)}, bf16...) custom-call(bf16[2,128,8,128]{3,2,1,0:T(8,128)(2,1)} %less_row.1, ...), custom_call_target="tpu_custom_call" | custom-call | flops 4000000000 | bytes 8388608 | tf_op jit(solution)/shard_map/pallas_call | solution.py:567
  90.5 0.0 copy-done.18
  90.5 0.0 copy-done.17
  90.6 0.0 copy-done.19
  90.6 0.0 copy-done.20
  90.6 1.6 %conditional.1 = ((bf16[2,128,8,128]{3,2,1,0:T(8,128)(2,1)}, bf16[2,128,8,128]{3,2,1,0:T(8,128)(2,1)}, bf16[2,128,8,128]{3,2,1,0:T(8,128)(2,1)}, bf16[2,128,8,128]{3,2,1,0:T(8,128)(2,1)}, f32[2,128,128]{2,1,0:T(8,128)})) conditional(s32[]{:T(128)} %bitcast.153, (f32[128,128]{1,0:T(8,128)S(1)}, f32[2,128,128]{2,1,0:T(8,128)}, ...), branch_computations={%region_0.11_spmd, %region_9.12_spmd} | conditional | flops 3422454784 | bytes 163476960 | solution.py:606
  90.8 1.4 %branch_1_fun.1 = (bf16[2,128,8,128]{3,2,1,0:T(8,128)(2,1)}, bf16[2,128,8,128]{3,2,1,0:T(8,128)(2,1)}, bf16[2,128,8,128]{3,2,1,0:T(8,128)(2,1)}, bf16[2,128,8,128]{3,2,1,0:T(8,128)(2,1)}, f32[2,128,128]{2,1,0:T(8,128)}) custom-call(bf16[2,128,8,128]{3,2,1,0:T(8,128)(2,1)S(1)} %get-tuple-element.30.refs_0_, ...), custom_call_target="tpu_custom_call" | custom-call | tf_op jit(solution)/shard_map/cond/branch_1_fun/pallas_call | solution.py:608
Async XLA Ops:
  0.6 89.9 %copy-start.18 = (bf16[2,128,8,128]{3,2,1,0:T(8,128)(2,1)S(1)}, bf16[2,128,8,128]{3,2,1,0:T(8,128)(2,1)}, u32[]{:S(2)}) copy-start(bf16[2,128,8,128]{3,2,1,0:T(8,128)(2,1)} %less_col.1) | copy-start | bytes 1572868
  0.6 89.9 %copy-start.17 = (bf16[2,128,8,128]{3,2,1,0:T(8,128)(2,1)S(1)}, bf16[2,128,8,128]{3,2,1,0:T(8,128)(2,1)}, u32[]{:S(2)}) copy-start(bf16[2,128,8,128]{3,2,1,0:T(8,128)(2,1)} %great_row.1) | copy-start | bytes 1572868
  0.7 89.9 %copy-start.19 = (bf16[2,128,8,128]{3,2,1,0:T(8,128)(2,1)S(1)}, bf16[2,128,8,128]{3,2,1,0:T(8,128)(2,1)}, u32[]{:S(2)}) copy-start(bf16[2,128,8,128]{3,2,1,0:T(8,128)(2,1)} %great_col.1) | copy-start | bytes 1572868
  0.7 89.9 %copy-start.20 = (f32[128,128]{1,0:T(8,128)S(1)}, f32[128,128]{1,0:T(8,128)}, u32[]{:S(2)}) copy-start(f32[128,128]{1,0:T(8,128)} %ham_ref.1) | copy-start | bytes 196612
